TPU v7x, 32 devices: a whole 2x2x4 slice. The times are simulated.
32 devices in a mesh: ctx: 8 (over y, x, core), tp: 4 (over z).
Axes of the slice: x: 2, y: 2, z: 4, core: 2. Of those that a mesh axis runs over, the one named last changes fastest.
Arguments:
- streams: bfloat16 [3, 2048, 2048], P(None, 'ctx', 'tp'), may hold values from -6 to 6
- short_filter: float32 [3, 7, 2048], P(None, None, 'tp'), may hold values from -2 to 2
- decay_rates: float32 [2048, 16], P('tp'), may hold values from 2.4414063e-05 to 0.05, as said below
- residues: float32 [2048, 16], P('tp'), may hold values from -0.06 to 0.06
- skip_gain: float32 [2048], P('tp'), may hold values from 0.5 to 1.5
- hyena_weight: bfloat16 [2048, 4096], P('tp'), may hold values from -0.1875 to 0.1875
- value_weight: bfloat16 [4096, 2048], P('tp'), may hold values from -0.125 to 0.125
- queries: bfloat16 [2048, 2048], P('ctx', 'tp'), may hold values from -16.5 to 16.5
- key_vectors: bfloat16 [2048, 2048], P('ctx', 'tp'), may hold values from -16.5 to 16.5
Outputs:
- hyena_out: bfloat16 [2048, 4096], P('ctx', 'tp')
- context: bfloat16 [2048, 2048], P('ctx', 'tp')
Inputs may be any that keep to these rules, and one draw needn't show every extreme that they name: `decay_rates`: decay rates lie between 1 / 40960 and 0.05.
All inputs are finite; a program needn't handle non-finite values.
Results may differ from a plain program's by a relative error of at most 0.0066.
Values may be sent and summed in bfloat16 or wider, within the bound.
A program may use at most 128 MiB of HBM per device.

v0:
```python
import math
import jax
import jax.numpy as jnp
from jax import lax
from jax.sharding import PartitionSpec as P

HD = 128


def from_behind(value, axis, steps):
    count = lax.axis_size(axis)
    initial, last = (max(0, -steps), min(count, count - steps))
    return lax.ppermute(value, axis, [(source, source + steps) for source in range(initial, last)])


def carried_in(value, axis, join, neutral):
    count, mine = (lax.axis_size(axis), lax.axis_index(axis))
    pieces = jax.tree.map(lambda part: lax.all_gather(part, axis), value)
    so_far = jax.tree.map(
        lambda part, zero: jnp.full_like(part, 0) + jnp.asarray(zero, part.dtype), value, neutral
    )

    def lap(position, so_far):
        longer = join(so_far, jax.tree.map(lambda part: part[position], pieces))
        return jax.tree.map(lambda new, old: jnp.where(position < mine, new, old), longer, so_far)

    return lax.fori_loop(0, count - 1, lap, so_far)


def chain_link(earlier, later):
    return (earlier[0] * later[0], later[0] * earlier[1] + later[1])


def hyena_mixer(streams, short_filter, decay_rates, residues, skip_gain, hyena_weight):
    tok_rows = streams.shape[1]
    previous = from_behind(streams[:, tok_rows - 6 :, :], "ctx", 1)
    extended = jnp.concatenate([previous, streams], axis=1).astype(jnp.float32)
    filtered = jnp.zeros((3, tok_rows, streams.shape[2]), jnp.float32)
    for offset in range(7):
        filtered = (
            filtered
            + short_filter[:, offset, None, :] * extended[:, 6 - offset : 6 - offset + tok_rows, :]
        )
    gate_part = filtered[0]
    product = filtered[1] * filtered[2]
    pole_state = product[:, :, None] * jnp.ones((1, 1, decay_rates.shape[1]), jnp.float32)
    stride = 1
    while stride < tok_rows:
        earlier_rows = jnp.pad(pole_state[: tok_rows - stride], ((stride, 0), (0, 0), (0, 0)))
        pole_state = pole_state + jnp.exp(-decay_rates * stride)[None] * earlier_rows
        stride = stride * 2
    end_state = pole_state[tok_rows - 1]
    block_decay = jnp.exp(-decay_rates * tok_rows)
    scanned = carried_in(
        (block_decay, end_state),
        "ctx",
        chain_link,
        (jnp.ones_like(block_decay), jnp.zeros_like(end_state)),
    )
    incoming = scanned[1]
    local_steps = (jnp.arange(tok_rows) + 1).astype(jnp.float32)
    pole_state = (
        pole_state + jnp.exp(-decay_rates[None] * local_steps[:, None, None]) * incoming[None]
    )
    longconv = jnp.sum(pole_state * residues[None], axis=2)
    gated = (gate_part * (longconv + skip_gain[None, :] * product)).astype(jnp.bfloat16)
    every_channel = lax.all_gather(gated, "tp", axis=1, tiled=True)
    column_rows = lax.all_to_all(hyena_weight, "tp", split_axis=1, concat_axis=0, tiled=True)
    summed = jnp.dot(every_channel, column_rows, preferred_element_type=jnp.float32)
    return summed.astype(jnp.bfloat16)


def attend_block(running, key_block, value_block, key_start, query_heads, query_index):
    rows_here = key_block.shape[0]
    head_count = query_heads.shape[1]
    scale = 1.0 / math.sqrt(HD)
    key_heads = key_block.reshape(rows_here, head_count, HD)
    value_heads = value_block.reshape(rows_here, head_count, HD)
    scores = (
        jnp.einsum("qhd,khd->hqk", query_heads, key_heads, preferred_element_type=jnp.float32)
        * scale
    )
    key_index = key_start + jnp.arange(rows_here)
    allowed = (key_index[None, :] <= query_index[:, None])[None]
    top_old, total_old, summed_old = running
    top_new = jnp.maximum(top_old, jnp.max(jnp.where(allowed, scores, -1e30), axis=2))
    weights = jnp.where(allowed, jnp.exp(scores - top_new[:, :, None]), 0.0)
    rescale = jnp.exp(top_old - top_new)
    total_new = total_old * rescale + jnp.sum(weights, axis=2)
    added = jnp.einsum(
        "hqk,khd->hqd",
        weights.astype(jnp.bfloat16),
        value_heads,
        preferred_element_type=jnp.float32,
    )
    return (top_new, total_new, summed_old * rescale[:, :, None] + added)


def fold_piece(running, key_piece, value_piece, step_fn):
    piece_rows = key_piece.shape[0]
    block_total = piece_rows // 512
    key_blocks = key_piece.reshape(block_total, 512, key_piece.shape[1])
    value_blocks = value_piece.reshape(block_total, 512, value_piece.shape[1])
    block_starts = 512 * jnp.arange(block_total)

    def scan_step(state_now, inputs):
        return (step_fn(state_now, inputs[0], inputs[1], inputs[2]), None)

    result, unused = lax.scan(scan_step, running, (key_blocks, value_blocks, block_starts))
    return result


def start_state(head_count, rows):
    return (
        jnp.full((head_count, rows), -1e30, jnp.float32),
        jnp.zeros((head_count, rows), jnp.float32),
        jnp.zeros((head_count, rows, HD), jnp.float32),
    )


def finish_state(state):
    top_final, total_final, summed_final = state
    rows = summed_final.shape[1]
    normalized = summed_final / total_final[:, :, None]
    return (
        normalized.transpose(1, 0, 2).reshape(rows, summed_final.shape[0] * HD).astype(jnp.bfloat16)
    )


def causal_attention(queries, key_vectors, values):
    tok_rows = queries.shape[0]
    head_count = queries.shape[1] // HD
    position = lax.axis_index("ctx")
    query_heads = queries.reshape(tok_rows, head_count, HD)
    query_index = position * tok_rows + jnp.arange(tok_rows)

    def step_fn(state_now, key_block, value_block, key_start):
        return attend_block(state_now, key_block, value_block, key_start, query_heads, query_index)

    initial = start_state(head_count, tok_rows)
    final_state = fold_piece(
        initial,
        lax.all_gather(key_vectors, "ctx", axis=0, tiled=True),
        lax.all_gather(values, "ctx", axis=0, tiled=True),
        step_fn,
    )
    return finish_state(final_state)


def shards(
    streams,
    short_filter,
    decay_rates,
    residues,
    skip_gain,
    hyena_weight,
    value_weight,
    queries,
    key_vectors,
):
    hyena_out = hyena_mixer(streams, short_filter, decay_rates, residues, skip_gain, hyena_weight)
    value_terms = jnp.dot(hyena_out, value_weight, preferred_element_type=jnp.float32)
    values = lax.psum_scatter(value_terms, "tp", scatter_dimension=1, tiled=True).astype(
        jnp.bfloat16
    )
    context = causal_attention(queries, key_vectors, values)
    return (hyena_out, context)


def solution(mesh):
    return jax.shard_map(
        shards,
        mesh=mesh,
        in_specs=(
            P(None, "ctx", "tp"),
            P(None, None, "tp"),
            P("tp", None),
            P("tp", None),
            P("tp"),
            P("tp", None),
            P("tp", None),
            P("ctx", "tp"),
            P("ctx", "tp"),
        ),
        out_specs=(P("ctx", "tp"), P("ctx", "tp")),
        check_vma=False,
    )
```

profile of v0, /device:TPU:0, one launch (start us, length us, event | category | flops | bytes accessed | tf_op | source)
XLA Modules:
  0.0 314.8 jit_solution(2053255607246101564)
XLA Ops:
  8.8 2.5 collective-permute-start
  11.3 6.5 %copy.36 = bf16[512,4096]{0,1:T(8,128)(2,1)} copy(bf16[512,4096]{1,0:T(8,128)(2,1)} %param.18) | data formatting | bytes 8388608 | tf_op args[5]
  17.8 5.7 %all-to-all-start = ((bf16[512,4,1024]{0,2,1:T(8,128)(2,1)}), bf16[512,4,1024]{0,2,1:T(8,128)(2,1)}, u32[]{:S(2)}, u32[]{:S(2)}) async-start(bf16[512,4,1024]{0,2,1:T(8,128)(2,1)} %bitcast.99), calls=%async_computation | async-start | bytes 8388608 | tf_op jit(solution)/shard_map/all_to_all | solution.py:68
  23.7 10.0 %all-gather = f32[4096,16]{0,1:T(8,128)S(1)} all-gather(f32[512,16]{0,1:T(8,128)S(1)} %get-tuple-element.290), channel_id=2, replica_groups=mesh['ctx'=8,'tp'=4] {'ctx'}, dimensions={0}, use_global_device_ids=true | all-gather | bytes 294912 | tf_op jit(solution)/shard_map/all_gather | solution.py:18
  37.7 4.7 %multiply_add_fusion.7 = f32[256,512,16]{1,2,0:T(8,128)} fusion(f32[255,512,16]{1,2,0:T(8,128)S(1)} %mul.299, f32[512,16]{0,1:T(8,128)S(1)} %get-tuple-element.282, f32[256,512]{1,0:T(8,128)S(1)} %fusion.37), kind=kLoop, calls=%fused_computation.38 | loop fusion | flops 4194304 | bytes 17301504 | tf_op jit(solution)/shard_map/add | solution.py:50
  42.4 4.4 %slice.125 = f32[254,512,16]{1,2,0:T(8,128)S(1)} slice(f32[256,512,16]{1,2,0:T(8,128)} %multiply_add_fusion.7), slice={[0:254], [0:512], [0:16]} | slice | bytes 16646144 | tf_op jit(solution)/shard_map/slice | solution.py:49
  46.9 4.7 %multiply_add_fusion.6 = f32[256,512,16]{1,2,0:T(8,128)} fusion(f32[254,512,16]{1,2,0:T(8,128)S(1)} %slice.125, f32[512,16]{0,1:T(8,128)S(1)} %get-tuple-element.283, f32[255,512,16]{1,2,0:T(8,128)S(1)} %mul.299, f32[512,16]{0,1:T(8,128)S(1)} %get-tuple-element.282, f32[256,512]{1,0:T(8,128)S(1)} %fusion.37), kind=kLoop, calls=%fused_computation.37 | loop fusion | flops 8388608 | bytes 25657344 | tf_op jit(solution)/shard_map/add | solution.py:50
  51.6 8.4 %slice.126 = f32[252,512,16]{1,2,0:T(8,128)} slice(f32[256,512,16]{1,2,0:T(8,128)} %multiply_add_fusion.6), slice={[0:252], [0:512], [0:16]} | slice | bytes 16515072 | tf_op jit(solution)/shard_map/slice | solution.py:49
  60.0 7.4 %multiply_add_fusion.5 = f32[256,512,16]{1,2,0:T(8,128)} fusion(f32[252,512,16]{1,2,0:T(8,128)} %slice.126, f32[512,16]{0,1:T(8,128)S(1)} %get-tuple-element.284, f32[254,512,16]{1,2,0:T(8,128)S(1)} %slice.125, f32[512,16]{0,1:T(8,128)S(1)} %get-tuple-element.283, f32[255,512,16]{1,2,0:T(8,128)S(1)} %mul.299, f32[512,16]{0,1:T(8,128)S(1)} %get-tuple-element.282, ...), kind=kLoop, calls=%fused_computation.36 | loop fusion | flops 12582912 | bytes 33947648 | tf_op jit(solution)/shard_map/add | solution.py:50
  67.4 8.3 %slice.127 = f32[248,512,16]{1,2,0:T(8,128)} slice(f32[256,512,16]{1,2,0:T(8,128)} %multiply_add_fusion.5), slice={[0:248], [0:512], [0:16]} | slice | bytes 16252928 | tf_op jit(solution)/shard_map/slice | solution.py:49
  75.7 12.1 %multiply_add_fusion.4 = f32[256,512,16]{1,2,0:T(8,128)} fusion(f32[256,512,16]{1,2,0:T(8,128)} %multiply_add_fusion.5, f32[248,512,16]{1,2,0:T(8,128)} %slice.127, f32[512,16]{0,1:T(8,128)S(1)} %get-tuple-element.285), kind=kLoop, calls=%fused_computation.35 | loop fusion | flops 4194304 | bytes 24936448 | tf_op jit(solution)/shard_map/add | solution.py:50
  87.8 8.1 %slice.128 = f32[240,512,16]{1,2,0:T(8,128)} slice(f32[256,512,16]{1,2,0:T(8,128)} %multiply_add_fusion.4), slice={[0:240], [0:512], [0:16]} | slice | bytes 15728640 | tf_op jit(solution)/shard_map/slice | solution.py:49
  95.9 12.0 %multiply_add_fusion.3 = f32[256,512,16]{1,2,0:T(8,128)} fusion(f32[256,512,16]{1,2,0:T(8,128)} %multiply_add_fusion.4, f32[240,512,16]{1,2,0:T(8,128)} %slice.128, f32[512,16]{0,1:T(8,128)S(1)} %get-tuple-element.286), kind=kLoop, calls=%fused_computation.34 | loop fusion | flops 4194304 | bytes 24674304 | tf_op jit(solution)/shard_map/add | solution.py:50
  107.8 7.7 %slice.129 = f32[224,512,16]{1,2,0:T(8,128)} slice(f32[256,512,16]{1,2,0:T(8,128)} %multiply_add_fusion.3), slice={[0:224], [0:512], [0:16]} | slice | bytes 14680064 | tf_op jit(solution)/shard_map/slice | solution.py:49
  115.5 11.7 %multiply_add_fusion.2 = f32[256,512,16]{1,2,0:T(8,128)} fusion(f32[256,512,16]{1,2,0:T(8,128)} %multiply_add_fusion.3, f32[224,512,16]{1,2,0:T(8,128)} %slice.129, f32[512,16]{0,1:T(8,128)S(1)} %get-tuple-element.287), kind=kLoop, calls=%fused_computation.33 | loop fusion | flops 4194304 | bytes 24150016 | tf_op jit(solution)/shard_map/add | solution.py:50
  127.3 2.8 slice-done
  130.1 8.7 %multiply_add_fusion.1 = f32[256,512,16]{1,2,0:T(8,128)} fusion(f32[256,512,16]{1,2,0:T(8,128)} %multiply_add_fusion.2, f32[192,512,16]{1,2,0:T(8,128)S(1)} %slice-done, f32[512,16]{0,1:T(8,128)S(1)} %get-tuple-element.288), kind=kLoop, calls=%fused_computation.32 | loop fusion | flops 4194304 | bytes 23101440 | tf_op jit(solution)/shard_map/add | solution.py:50
  138.8 2.2 slice-done.1
  141.0 8.9 %multiply_add_fusion = f32[256,512,16]{1,2,0:T(8,128)} fusion(f32[256,512,16]{1,2,0:T(8,128)} %multiply_add_fusion.1, f32[128,512,16]{1,2,0:T(8,128)S(1)} %slice-done.1, f32[512,16]{0,1:T(8,128)S(1)} %get-tuple-element.289), kind=kLoop, calls=%fused_computation.31 | loop fusion | flops 4194304 | bytes 21004288 | tf_op jit(solution)/shard_map/add | solution.py:50
  150.8 8.9 %all_gather.20 = f32[8,512,16]{1,2,0:T(8,128)S(1)} all-gather(f32[1,512,16]{1,2,0:T(8,128)S(1)} %slice.132), channel_id=1, replica_groups=mesh['ctx'=8,'tp'=4] {'ctx'}, dimensions={0}, use_global_device_ids=true | all-gather | bytes 294912 | tf_op jit(solution)/shard_map/all_gather | solution.py:18
  160.2 5.2 %multiply_reduce_fusion = f32[256,512]{1,0:T(8,128)S(1)} fusion(f32[256,512,16]{1,2,0:T(8,128)} %multiply_add_fusion, f32[512,16]{0,1:T(8,128)S(1)} %copy-done.5, f32[512,16]{0,1:T(8,128)S(1)} %get-tuple-element.144, f32[256]{0:T(256)S(1)} %add_convert_fusion, f32[512,16]{0,1:T(8,128)S(1)} %get-tuple-element.281), kind=kLoop, calls=%fused_computation.30 | loop fusion | flops 10354688 | bytes 9012224 | tf_op jit(solution)/shard_map/reduce_sum | solution.py:65
  166.4 6.3 %copy.37 = bf16[4,512,1024]{2,1,0:T(8,128)(2,1)} copy(bf16[4,512,1024]{1,2,0:T(8,128)(2,1)} %bitcast.4) | data formatting | bytes 8388608 | tf_op jit(solution)/shard_map/all_to_all | solution.py:68
  172.7 22.1 %all-gather.5.cloned.1.call-done = bf16[256,2048]{1,0:T(8,128)(2,1)} async-done(((bf16[256,512]{1,0:T(8,128)(2,1)}), bf16[256,2048]{1,0:T(8,128)(2,1)}) %all-gather.5.cloned.1.call-update) | async-done | bytes 1048592 | tf_op jit(solution)/shard_map/all_gather | solution.py:67
  194.9 3.8 %convolution_convert_fusion = bf16[256,1024]{1,0:T(8,128)(2,1)S(1)} fusion(bf16[256,2048]{1,0:T(8,128)(2,1)} %all-gather.5.cloned.1.call-done, bf16[2048,1024]{1,0:T(8,128)(2,1)} %bitcast.101), kind=kOutput, calls=%fused_computation.52 | convolution fusion | flops 1074003968 | bytes 5767168 | tf_op jit(solution)/shard_map/dot_general | solution.py:69
  199.5 4.8 %fusion.29 = f32[256,2048]{1,0:T(8,128)} fusion(bf16[256,1024]{1,0:T(8,128)(2,1)S(1)} %convolution_convert_fusion, bf16[1024,2048]{1,0:T(8,128)(2,1)} %param.19), kind=kOutput, calls=%fused_computation.82 | convolution fusion | flops 1073741824 | bytes 6815744 | tf_op jit(solution)/shard_map/dot_general | solution.py:162
  204.9 42.9 %reduce-scatter.2.cloned.1.call-done = f32[256,512]{1,0:T(8,128)} async-done(((f32[256,2048]{1,0:T(8,128)}), f32[256,512]{1,0:T(8,128)}) %reduce-scatter.2.cloned.1.call-update) | async-done | bytes 524304 | tf_op jit(solution)/shard_map/reduce_scatter | solution.py:163
  250.4 26.3 %all-gather.9.cloned.1.call-done = bf16[2048,512]{1,0:T(8,128)(2,1)} async-done(((bf16[256,512]{1,0:T(8,128)(2,1)}), bf16[2048,512]{1,0:T(8,128)(2,1)}) %all-gather.9.cloned.1.call-update) | async-done | bytes 2097168 | tf_op jit(solution)/shard_map/all_gather | solution.py:144
  276.7 28.8 %while.30 = (s32[]{:T(128)}, f32[4,256]{1,0:T(4,128)S(1)}, f32[4,256]{1,0:T(4,128)S(1)}, f32[4,256,128]{2,1,0:T(8,128)}, s32[4]{0:T(128)}, /*index=5*/bf16[4,512...) while((s32[]{:T(128)}, f32[4,256]{1,0:T(4,128)S(1)}, ...), condition=%wide.region_7.8_spmd.clone, body=%wide.region_4.7_spmd.clone.sunk | while | flops 274732800 | bytes 13441169 | solution.py:109
  287.9 2.6 convolution_add_fusion.2
  295.4 2.6 convolution_add_fusion.2
  302.8 2.6 convolution_add_fusion.2
  305.5 2.0 copy_bitcast_fusion.1
  (120 shorter events, 32.2 us)
Async XLA Ops:
  8.7 14.8 %copy-start.4 = (f32[3,7,512]{2,1,0:T(8,128)S(1)}, f32[3,7,512]{2,1,0:T(8,128)}, u32[]{:S(2)}) copy-start(f32[3,7,512]{2,1,0:T(8,128)} %param.14) | copy-start | bytes 129028
  8.8 14.8 %copy-start.6 = (f32[512,16]{0,1:T(8,128)S(1)}, f32[512,16]{0,1:T(8,128)}, u32[]{:S(2)}) copy-start(f32[512,16]{0,1:T(8,128)} %param.15) | copy-start | bytes 98308
  8.8 25.1 %copy-start.2 = (bf16[3,256,512]{2,1,0:T(8,128)(2,1)S(1)}, bf16[3,256,512]{2,1,0:T(8,128)(2,1)}, u32[]{:S(2)}) copy-start(bf16[3,256,512]{2,1,0:T(8,128)(2,1)} %param.13) | copy-start | bytes 2359300
  8.8 25.1 %collective-permute-start = (bf16[3,6,512]{2,1,0:T(8,128)(2,1)S(1)}, bf16[3,6,512]{2,1,0:T(8,128)(2,1)S(1)}, u32[]{:S(2)}, u32[]{:S(2)}) collective-permute-start(bf16[3,6,512]{2,1,0:T(8,128)(2,1)S(1)} %slice.87), channel_id=1, source_target_pairs={{0,4},{4,8},{8,12},{12,16},{16,20},{20,24},{24,28},{1,5},{5,9},{9,... | collective-permute-start | bytes 55304 | tf_op jit(solution)/shard_map/ppermute | solution.py:13
  17.8 148.6 %all-to-all-start = ((bf16[512,4,1024]{0,2,1:T(8,128)(2,1)}), bf16[512,4,1024]{0,2,1:T(8,128)(2,1)}, u32[]{:S(2)}, u32[]{:S(2)}) async-start(bf16[512,4,1024]{0,2,1:T(8,128)(2,1)} %bitcast.99), calls=%async_computation | async-start | bytes 8388608 | tf_op jit(solution)/shard_map/all_to_all | solution.py:68
  23.5 171.4 %all-gather.5.cloned.1.call-start = ((), (), s32[]{:S(2)}) async-start(), calls=%async_computation.2 | async-start | bytes 1310720 | tf_op jit(solution)/shard_map/all_gather | solution.py:67
  35.4 1.2 copy-start
  127.3 2.8 slice-start
  138.8 2.2 slice-start.1
  141.0 19.2 %copy-start.5 = (f32[512,16]{0,1:T(8,128)S(1)}, f32[512,16]{0,1:T(8,128)}, u32[]{:S(2)}) copy-start(f32[512,16]{0,1:T(8,128)} %param.16) | copy-start | bytes 98308
  149.9 15.5 %copy-start.1 = (f32[3,256,512]{2,1,0:T(8,128)S(1)}, f32[3,256,512]{2,1,0:T(8,128)}, u32[]{:S(2)}) copy-start(f32[3,256,512]{2,1,0:T(8,128)} %copy-done) | copy-start | bytes 4718596
  149.9 15.5 %copy-start.7 = (f32[512]{0:T(512)S(1)}, f32[512]{0:T(512)}, u32[]{:S(2)}) copy-start(f32[512]{0:T(512)} %param.17) | copy-start | bytes 6148
  166.4 81.4 %reduce-scatter.2.cloned.1.call-start = ((), (), s32[]{:S(2)}) async-start(), calls=%async_computation.4 | async-start | bytes 2621440 | tf_op jit(solution)/shard_map/reduce_scatter | solution.py:163
  194.9 54.7 %copy-start.3 = (bf16[256,512]{1,0:T(8,128)(2,1)S(1)}, bf16[256,512]{1,0:T(8,128)(2,1)}, u32[]{:S(2)}) copy-start(bf16[256,512]{1,0:T(8,128)(2,1)} %param.20) | copy-start | bytes 786436
  198.7 0.8 copy-start.8
  204.2 46.2 %all-gather.7.cloned.1.call-start = ((), (), s32[]{:S(2)}) async-start(), calls=%async_computation.3 | async-start | bytes 2359296 | tf_op jit(solution)/shard_map/all_gather | solution.py:143
  204.8 71.9 %all-gather.9.cloned.1.call-start = ((), (), s32[]{:S(2)}) async-start(), calls=%async_computation.5 | async-start | bytes 2359296 | tf_op jit(solution)/shard_map/all_gather | solution.py:144
Sparse Core Ops, SparseCore 0:
  166.5 28.3 all-gather.4
  204.4 43.3 reduce-scatter.1
Sparse Core Ops, SparseCore 1:
  206.6 27.2 all-gather.6
  249.6 27.0 all-gather.8
where the time goes:
time: 316 us; the launch traced here: 315 us
  waiting for transfers between devices  91.8 us (29%)
  other arithmetic  87.6 us (28%)
  local copies, waits for them, and re-layouts  71.7 us (23%)
  matrix products  20.3 us (6%)
  blocking collectives  18.9 us (6%)
  between operations  15.8 us (5%)
  starting transfers between devices  8.32 us (3%)
    add x8, other arithmetic, hyena_mixer(): pole_state + jnp.exp(-decay_rates * stride)[None] * earlier_rows  70.3 us
    reduce_scatter x1, waiting for transfers between devices, shards(): lax.psum_scatter(value_terms, 'tp', scatter_dimension=1, tiled=True)  42.9 us
    slice x10, local copies, waits for them, and re-layouts, hyena_mixer(): pole_state[:tok_rows - stride]  42 us
    all_gather x1, waiting for transfers between devices, causal_attention(): lax.all_gather(values, 'ctx', axis=0, tiled=True)  26.3 us
    all_gather x1, waiting for transfers between devices, hyena_mixer(): every_channel = lax.all_gather(gated, 'tp', axis=1, tiled=True)  22.1 us
    all_gather x2, blocking collectives, carried_in(): pieces = jax.tree.map(lambda part: lax.all_gather(part, axis), value)  18.9 us
    dynamic_slice x16, local copies, waits for them, and re-layouts, fold_piece(): lax.scan(scan_step, running, (key_blocks, value_blocks, block_starts))  11.7 us
    dot_general x4, matrix products, attend_block(): jnp.einsum('hqk,khd->hqd', weights.astype(jnp.bfloat16), value_heads, pre...  9.45 us
  transfers between devices with their start and end apart: 6, of which 3 were waited for; matrix products, arithmetic and copies ran while one was open for 42% of the time, Pallas kernels for 0%

commit v1 on v0

--- a/solution.py
+++ b/solution.py
@@ -65,7 +65,9 @@
     longconv = jnp.sum(pole_state * residues[None], axis=2)
     gated = (gate_part * (longconv + skip_gain[None, :] * product)).astype(jnp.bfloat16)
     every_channel = lax.all_gather(gated, "tp", axis=1, tiled=True)
-    column_rows = lax.all_to_all(hyena_weight, "tp", split_axis=1, concat_axis=0, tiled=True)
+    parts = jnp.split(hyena_weight, lax.axis_size("tp"), axis=1)
+    incoming_2 = lax.all_to_all(jnp.stack(parts), "tp", 0, 0)
+    column_rows = jnp.concatenate(incoming_2, axis=0)
     summed = jnp.dot(every_channel, column_rows, preferred_element_type=jnp.float32)
     return summed.astype(jnp.bfloat16)
 

time: 316 us -> 311 us (0.984)
  local copies, waits for them, and re-layouts: 71.7 us -> 60.6 us
  waiting for transfers between devices: 91.8 us -> 98.1 us
    unnamed x26 -> x27, local copies, waits for them, and re-layouts: 8.86 us -> 1.3 us
    all_gather x1, waiting for transfers between devices: 22.1 us -> 28.4 us  [hyena_mixer(): every_channel = lax.all_gather(gated, 'tp', axis=1, tiled=True)]
    all_to_all x1 -> x0, local copies, waits for them, and re-layouts: 6.31 us -> none  [hyena_mixer(): lax.all_to_all(hyena_weight, 'tp', split_axis=1, concat_axis=0, tiled=True)]
  transfers between devices with their start and end apart: 6 -> 6, of which waited for: 3 -> 3; matrix products, arithmetic and copies ran while one was open for 42% -> 40% of each run, Pallas kernels for 0% -> 0%
where the time goes in v1:
time: 311 us; the launch traced here: 310 us
  waiting for transfers between devices  98.1 us (32%)
  other arithmetic  89.9 us (29%)
  local copies, waits for them, and re-layouts  60.6 us (19%)
  blocking collectives  18.9 us (6%)
  matrix products  18.3 us (6%)
  between operations  15.8 us (5%)
  starting transfers between devices  8.31 us (3%)
    add x8, other arithmetic, hyena_mixer(): pole_state + jnp.exp(-decay_rates * stride)[None] * earlier_rows  70.3 us
    reduce_scatter x1, waiting for transfers between devices, shards(): lax.psum_scatter(value_terms, 'tp', scatter_dimension=1, tiled=True)  42.9 us
    slice x10, local copies, waits for them, and re-layouts, hyena_mixer(): pole_state[:tok_rows - stride]  42 us
    all_gather x1, waiting for transfers between devices, hyena_mixer(): every_channel = lax.all_gather(gated, 'tp', axis=1, tiled=True)  28.4 us
    all_gather x1, waiting for transfers between devices, causal_attention(): lax.all_gather(values, 'ctx', axis=0, tiled=True)  26.2 us
    all_gather x2, blocking collectives, carried_in(): pieces = jax.tree.map(lambda part: lax.all_gather(part, axis), value)  18.9 us
    dynamic_slice x16, local copies, waits for them, and re-layouts, fold_piece(): lax.scan(scan_step, running, (key_blocks, value_blocks, block_starts))  11.8 us
    dot_general x4, matrix products, attend_block(): jnp.einsum('hqk,khd->hqd', weights.astype(jnp.bfloat16), value_heads, pre...  9.48 us
  transfers between devices with their start and end apart: 6, of which 3 were waited for; matrix products, arithmetic and copies ran while one was open for 40% of the time, Pallas kernels for 0%

profile of v1, /device:TPU:0, one launch (start us, length us, event | category | flops | bytes accessed | tf_op | source)
XLA Modules:
  0.0 310.3 jit_solution(11247980995794421684)
XLA Ops:
  8.7 2.4 collective-permute-start
  11.1 2.6 slice_bitcast_fusion.3
  13.7 2.2 pad_maximum_fusion
  16.0 5.8 %all-to-all-start = ((bf16[4,512,1024]{2,1,0:T(8,128)(2,1)}), bf16[4,512,1024]{2,1,0:T(8,128)(2,1)}, u32[]{:S(2)}, u32[]{:S(2)}) async-start(bf16[4,512,1024]{2,1,0:T(8,128)(2,1)} %pad_maximum_fusion), calls=%async_computation | async-start | bytes 8388608 | tf_op jit(solution)/shard_map/all_to_all | solution.py:69
  22.0 10.0 %all-gather = f32[4096,16]{0,1:T(8,128)S(1)} all-gather(f32[512,16]{0,1:T(8,128)S(1)} %get-tuple-element.294), channel_id=2, replica_groups=mesh['ctx'=8,'tp'=4] {'ctx'}, dimensions={0}, use_global_device_ids=true | all-gather | bytes 294912 | tf_op jit(solution)/shard_map/all_gather | solution.py:18
  35.0 4.7 %multiply_add_fusion.7 = f32[256,512,16]{1,2,0:T(8,128)} fusion(f32[255,512,16]{1,2,0:T(8,128)S(1)} %mul.299, f32[512,16]{0,1:T(8,128)S(1)} %get-tuple-element.286, f32[256,512]{1,0:T(8,128)S(1)} %fusion.37), kind=kLoop, calls=%fused_computation.38 | loop fusion | flops 4194304 | bytes 17301504 | tf_op jit(solution)/shard_map/add | solution.py:50
  39.8 4.4 %slice.125 = f32[254,512,16]{1,2,0:T(8,128)S(1)} slice(f32[256,512,16]{1,2,0:T(8,128)} %multiply_add_fusion.7), slice={[0:254], [0:512], [0:16]} | slice | bytes 16646144 | tf_op jit(solution)/shard_map/slice | solution.py:49
  44.2 4.7 %multiply_add_fusion.6 = f32[256,512,16]{1,2,0:T(8,128)} fusion(f32[254,512,16]{1,2,0:T(8,128)S(1)} %slice.125, f32[512,16]{0,1:T(8,128)S(1)} %get-tuple-element.287, f32[255,512,16]{1,2,0:T(8,128)S(1)} %mul.299, f32[512,16]{0,1:T(8,128)S(1)} %get-tuple-element.286, f32[256,512]{1,0:T(8,128)S(1)} %fusion.37), kind=kLoop, calls=%fused_computation.37 | loop fusion | flops 8388608 | bytes 25657344 | tf_op jit(solution)/shard_map/add | solution.py:50
  48.9 8.4 %slice.126 = f32[252,512,16]{1,2,0:T(8,128)} slice(f32[256,512,16]{1,2,0:T(8,128)} %multiply_add_fusion.6), slice={[0:252], [0:512], [0:16]} | slice | bytes 16515072 | tf_op jit(solution)/shard_map/slice | solution.py:49
  57.3 7.4 %multiply_add_fusion.5 = f32[256,512,16]{1,2,0:T(8,128)} fusion(f32[252,512,16]{1,2,0:T(8,128)} %slice.126, f32[512,16]{0,1:T(8,128)S(1)} %get-tuple-element.288, f32[254,512,16]{1,2,0:T(8,128)S(1)} %slice.125, f32[512,16]{0,1:T(8,128)S(1)} %get-tuple-element.287, f32[255,512,16]{1,2,0:T(8,128)S(1)} %mul.299, f32[512,16]{0,1:T(8,128)S(1)} %get-tuple-element.286, ...), kind=kLoop, calls=%fused_computation.36 | loop fusion | flops 12582912 | bytes 33947648 | tf_op jit(solution)/shard_map/add | solution.py:50
  64.8 8.3 %slice.127 = f32[248,512,16]{1,2,0:T(8,128)} slice(f32[256,512,16]{1,2,0:T(8,128)} %multiply_add_fusion.5), slice={[0:248], [0:512], [0:16]} | slice | bytes 16252928 | tf_op jit(solution)/shard_map/slice | solution.py:49
  73.1 12.1 %multiply_add_fusion.4 = f32[256,512,16]{1,2,0:T(8,128)} fusion(f32[256,512,16]{1,2,0:T(8,128)} %multiply_add_fusion.5, f32[248,512,16]{1,2,0:T(8,128)} %slice.127, f32[512,16]{0,1:T(8,128)S(1)} %get-tuple-element.289), kind=kLoop, calls=%fused_computation.35 | loop fusion | flops 4194304 | bytes 24936448 | tf_op jit(solution)/shard_map/add | solution.py:50
  85.1 8.1 %slice.128 = f32[240,512,16]{1,2,0:T(8,128)} slice(f32[256,512,16]{1,2,0:T(8,128)} %multiply_add_fusion.4), slice={[0:240], [0:512], [0:16]} | slice | bytes 15728640 | tf_op jit(solution)/shard_map/slice | solution.py:49
  93.2 12.0 %multiply_add_fusion.3 = f32[256,512,16]{1,2,0:T(8,128)} fusion(f32[256,512,16]{1,2,0:T(8,128)} %multiply_add_fusion.4, f32[240,512,16]{1,2,0:T(8,128)} %slice.128, f32[512,16]{0,1:T(8,128)S(1)} %get-tuple-element.290), kind=kLoop, calls=%fused_computation.34 | loop fusion | flops 4194304 | bytes 24674304 | tf_op jit(solution)/shard_map/add | solution.py:50
  105.2 7.7 %slice.129 = f32[224,512,16]{1,2,0:T(8,128)} slice(f32[256,512,16]{1,2,0:T(8,128)} %multiply_add_fusion.3), slice={[0:224], [0:512], [0:16]} | slice | bytes 14680064 | tf_op jit(solution)/shard_map/slice | solution.py:49
  112.9 11.7 %multiply_add_fusion.2 = f32[256,512,16]{1,2,0:T(8,128)} fusion(f32[256,512,16]{1,2,0:T(8,128)} %multiply_add_fusion.3, f32[224,512,16]{1,2,0:T(8,128)} %slice.129, f32[512,16]{0,1:T(8,128)S(1)} %get-tuple-element.291), kind=kLoop, calls=%fused_computation.33 | loop fusion | flops 4194304 | bytes 24150016 | tf_op jit(solution)/shard_map/add | solution.py:50
  124.6 2.8 slice-done
  127.4 8.7 %multiply_add_fusion.1 = f32[256,512,16]{1,2,0:T(8,128)} fusion(f32[256,512,16]{1,2,0:T(8,128)} %multiply_add_fusion.2, f32[192,512,16]{1,2,0:T(8,128)S(1)} %slice-done, f32[512,16]{0,1:T(8,128)S(1)} %get-tuple-element.292), kind=kLoop, calls=%fused_computation.32 | loop fusion | flops 4194304 | bytes 23101440 | tf_op jit(solution)/shard_map/add | solution.py:50
  136.2 2.2 slice-done.1
  138.4 8.9 %multiply_add_fusion = f32[256,512,16]{1,2,0:T(8,128)} fusion(f32[256,512,16]{1,2,0:T(8,128)} %multiply_add_fusion.1, f32[128,512,16]{1,2,0:T(8,128)S(1)} %slice-done.1, f32[512,16]{0,1:T(8,128)S(1)} %get-tuple-element.293), kind=kLoop, calls=%fused_computation.31 | loop fusion | flops 4194304 | bytes 21004288 | tf_op jit(solution)/shard_map/add | solution.py:50
  148.2 8.9 %all_gather.20 = f32[8,512,16]{1,2,0:T(8,128)S(1)} all-gather(f32[1,512,16]{1,2,0:T(8,128)S(1)} %slice.132), channel_id=1, replica_groups=mesh['ctx'=8,'tp'=4] {'ctx'}, dimensions={0}, use_global_device_ids=true | all-gather | bytes 294912 | tf_op jit(solution)/shard_map/all_gather | solution.py:18
  157.6 5.2 %multiply_reduce_fusion = f32[256,512]{1,0:T(8,128)S(1)} fusion(f32[256,512,16]{1,2,0:T(8,128)} %multiply_add_fusion, f32[512,16]{0,1:T(8,128)S(1)} %copy-done.5, f32[512,16]{0,1:T(8,128)S(1)} %get-tuple-element.144, f32[256]{0:T(256)S(1)} %add_convert_fusion, f32[512,16]{0,1:T(8,128)S(1)} %get-tuple-element.285), kind=kLoop, calls=%fused_computation.30 | loop fusion | flops 10354688 | bytes 9012224 | tf_op jit(solution)/shard_map/reduce_sum | solution.py:65
  163.8 28.4 %all-gather.5.cloned.1.call-done = bf16[256,2048]{1,0:T(8,128)(2,1)} async-done(((bf16[256,512]{1,0:T(8,128)(2,1)}), bf16[256,2048]{1,0:T(8,128)(2,1)}) %all-gather.5.cloned.1.call-update) | async-done | bytes 1048592 | tf_op jit(solution)/shard_map/all_gather | solution.py:67
  192.2 3.9 %convolution_convert_fusion = bf16[256,1024]{1,0:T(8,128)(2,1)S(1)} fusion(bf16[256,2048]{1,0:T(8,128)(2,1)} %all-gather.5.cloned.1.call-done, bf16[2048,1024]{1,0:T(8,128)(2,1)} %bitcast.7), kind=kOutput, calls=%fused_computation.53 | convolution fusion | flops 1074003968 | bytes 5767168 | tf_op jit(solution)/shard_map/dot_general | solution.py:71
  197.0 2.6 fusion.29
  200.2 42.9 %reduce-scatter.2.cloned.1.call-done = f32[256,512]{1,0:T(8,128)} async-done(((f32[256,2048]{1,0:T(8,128)}), f32[256,512]{1,0:T(8,128)}) %reduce-scatter.2.cloned.1.call-update) | async-done | bytes 524304 | tf_op jit(solution)/shard_map/reduce_scatter | solution.py:165
  245.8 26.2 %all-gather.9.cloned.1.call-done = bf16[2048,512]{1,0:T(8,128)(2,1)} async-done(((bf16[256,512]{1,0:T(8,128)(2,1)}), bf16[2048,512]{1,0:T(8,128)(2,1)}) %all-gather.9.cloned.1.call-update) | async-done | bytes 2097168 | tf_op jit(solution)/shard_map/all_gather | solution.py:146
  272.0 28.9 %while.30 = (s32[]{:T(128)}, f32[4,256]{1,0:T(4,128)S(1)}, f32[4,256]{1,0:T(4,128)S(1)}, f32[4,256,128]{2,1,0:T(8,128)}, s32[4]{0:T(128)}, /*index=5*/bf16[4,512...) while((s32[]{:T(128)}, f32[4,256]{1,0:T(4,128)S(1)}, ...), condition=%wide.region_7.8_spmd.clone, body=%wide.region_4.7_spmd.clone.sunk | while | flops 274732800 | bytes 13441169 | solution.py:111
  283.3 2.6 convolution_add_fusion.2
  290.8 2.6 convolution_add_fusion.2
  298.3 2.6 convolution_add_fusion.2
  301.0 2.0 copy_bitcast_fusion.1
  (122 shorter events, 31.4 us)
Async XLA Ops:
  8.7 23.4 %collective-permute-start = (bf16[3,6,512]{2,1,0:T(8,128)(2,1)S(1)}, bf16[3,6,512]{2,1,0:T(8,128)(2,1)S(1)}, u32[]{:S(2)}, u32[]{:S(2)}) collective-permute-start(bf16[3,6,512]{2,1,0:T(8,128)(2,1)S(1)} %slice.87), channel_id=1, source_target_pairs={{0,4},{4,8},{8,12},{12,16},{16,20},{20,24},{24,28},{1,5},{5,9},{9,... | collective-permute-start | bytes 55304 | tf_op jit(solution)/shard_map/ppermute | solution.py:13
  16.0 5.8 %copy-start.4 = (f32[3,7,512]{2,1,0:T(8,128)S(1)}, f32[3,7,512]{2,1,0:T(8,128)}, u32[]{:S(2)}) copy-start(f32[3,7,512]{2,1,0:T(8,128)} %param.14) | copy-start | bytes 129028
  16.0 5.9 %copy-start.6 = (f32[512,16]{0,1:T(8,128)S(1)}, f32[512,16]{0,1:T(8,128)}, u32[]{:S(2)}) copy-start(f32[512,16]{0,1:T(8,128)} %param.15) | copy-start | bytes 98308
  16.0 16.2 %copy-start.2 = (bf16[3,256,512]{2,1,0:T(8,128)(2,1)S(1)}, bf16[3,256,512]{2,1,0:T(8,128)(2,1)}, u32[]{:S(2)}) copy-start(bf16[3,256,512]{2,1,0:T(8,128)(2,1)} %param.13) | copy-start | bytes 2359300
  16.0 176.2 %all-to-all-start = ((bf16[4,512,1024]{2,1,0:T(8,128)(2,1)}), bf16[4,512,1024]{2,1,0:T(8,128)(2,1)}, u32[]{:S(2)}, u32[]{:S(2)}) async-start(bf16[4,512,1024]{2,1,0:T(8,128)(2,1)} %pad_maximum_fusion), calls=%async_computation | async-start | bytes 8388608 | tf_op jit(solution)/shard_map/all_to_all | solution.py:69
  21.8 170.4 %all-gather.5.cloned.1.call-start = ((), (), s32[]{:S(2)}) async-start(), calls=%async_computation.2 | async-start | bytes 1310720 | tf_op jit(solution)/shard_map/all_gather | solution.py:67
  33.7 1.3 copy-start
  124.6 2.8 slice-start
  136.2 2.2 slice-start.1
  138.4 19.3 %copy-start.5 = (f32[512,16]{0,1:T(8,128)S(1)}, f32[512,16]{0,1:T(8,128)}, u32[]{:S(2)}) copy-start(f32[512,16]{0,1:T(8,128)} %param.16) | copy-start | bytes 98308
  147.3 15.5 %copy-start.1 = (f32[3,256,512]{2,1,0:T(8,128)S(1)}, f32[3,256,512]{2,1,0:T(8,128)}, u32[]{:S(2)}) copy-start(f32[3,256,512]{2,1,0:T(8,128)} %copy-done) | copy-start | bytes 4718596
  147.3 15.5 %copy-start.7 = (f32[512]{0:T(512)S(1)}, f32[512]{0:T(512)}, u32[]{:S(2)}) copy-start(f32[512]{0:T(512)} %param.17) | copy-start | bytes 6148
  163.8 79.3 %reduce-scatter.2.cloned.1.call-start = ((), (), s32[]{:S(2)}) async-start(), calls=%async_computation.4 | async-start | bytes 2621440 | tf_op jit(solution)/shard_map/reduce_scatter | solution.py:165
  192.2 4.7 %copy-start.8 = (bf16[1024,2048]{1,0:T(8,128)(2,1)S(1)}, bf16[1024,2048]{1,0:T(8,128)(2,1)}, u32[]{:S(2)}) copy-start(bf16[1024,2048]{1,0:T(8,128)(2,1)} %param.19) | copy-start | bytes 12582916
  196.2 0.8 copy-start.9
  197.0 47.9 %copy-start.3 = (bf16[256,512]{1,0:T(8,128)(2,1)S(1)}, bf16[256,512]{1,0:T(8,128)(2,1)}, u32[]{:S(2)}) copy-start(bf16[256,512]{1,0:T(8,128)(2,1)} %param.20) | copy-start | bytes 786436
  199.6 46.2 %all-gather.7.cloned.1.call-start = ((), (), s32[]{:S(2)}) async-start(), calls=%async_computation.3 | async-start | bytes 2359296 | tf_op jit(solution)/shard_map/all_gather | solution.py:145
  200.1 71.9 %all-gather.9.cloned.1.call-start = ((), (), s32[]{:S(2)}) async-start(), calls=%async_computation.5 | async-start | bytes 2359296 | tf_op jit(solution)/shard_map/all_gather | solution.py:146
Sparse Core Ops, SparseCore 0:
  163.9 28.3 all-gather.4
  199.7 43.3 reduce-scatter.1
Sparse Core Ops, SparseCore 1:
  201.9 27.2 all-gather.6
  245.0 27.0 all-gather.8
